TPU v7x, 32 devices: a whole 2x2x4 slice. The times are simulated.
32 devices in a mesh: gx: 8 (over z, x), ma: 4 (over y, core).
Axes of the slice: x: 2, y: 2, z: 4, core: 2. Of those that a mesh axis runs over, the one named last changes fastest.
Arguments:
- solution: float32 [256, 8, 8, 256], P('ma', 'gx'), may hold values from -1.2 to 1.2
- source: float32 [256, 8, 8, 256], P('ma', 'gx'), may hold values from -6 to 6
- mean_conductivity: float32 [8, 8, 256], P('gx'), may hold values from 0.5 to 2
- kl_fields: float32 [10, 8, 8, 256], P(None, 'gx'), may hold values from -0.9 to 0.9
- couplings: int32 [10, 256, 2], replicated, may hold values from 0 to 255, as said below
- mode_index: int32 [256, 10], replicated, may hold values from 0 to 3, as said below
Outputs:
- residual: float32 [256, 8, 8, 256], P('ma', 'gx')
- correction: float32 [256, 8, 8, 256], P('ma', 'gx')
Inputs may be any that keep to these rules, and one draw needn't show every extreme that they name: couplings[k, i, 0] is the mode whose multi-index is mode_index[i] plus one in variable k, couplings[k, i, 1] the mode whose multi-index is mode_index[i] minus one in variable k; where no mode has that multi-index the entry is i itself. `mode_index`: the rows are 256 distinct multi-indices of total degree at most 3 in graded order: the total degree never falls with the mode number, all multi-indices of each total degree below 3 are present, and some mode has degree 3 in one variable; the order of the variables is drawn from the seed.
All inputs are finite; a program needn't handle non-finite values.
Results may differ from a plain program's by a relative error of at most 0.000071.
Values sent between devices are 32-bit elements; how exact they have to be, the bound alone decides.
A program may use at most 128 MiB of HBM per device.

v0:
```python
import jax
import jax.numpy as jnp
from jax import lax
from jax.sharding import PartitionSpec as P

STEPS = 3


def extended(array, sides, width):
    for axis, dim in sides:
        size, length = (lax.axis_size(axis), array.shape[dim])
        up = [(i, (i + 1) % size) for i in range(size)]
        down = [(j, i) for i, j in up]
        last = lax.slice_in_dim(array, length - width, length, axis=dim)
        initial = lax.slice_in_dim(array, 0, width, axis=dim)
        before = lax.ppermute(last, axis, up)
        after = lax.ppermute(initial, axis, down)
        array = jnp.concatenate([before, array, after], axis=dim)
    return array


def diffuse(coefficient, padded):
    center = coefficient[1:-1]
    values = padded[..., 1:-1, :, :]
    total = 0.5 * (center + coefficient[2:]) * (values - padded[..., 2:, :, :])
    total = total + 0.5 * (center + coefficient[:-2]) * (values - padded[..., :-2, :, :])
    for which_dim in (-2, -1):
        for offset in (-1, 1):
            total = total + 0.5 * (center + jnp.roll(center, offset, which_dim)) * (
                values - jnp.roll(values, offset, which_dim)
            )
    return total


def coupling_table(couplings, mode_index):
    modes_all = mode_index.shape[0]
    degrees = mode_index.astype(jnp.float32).T
    weight = jnp.sqrt(jnp.maximum(degrees[:, :, None], degrees[:, None, :]))
    columns = lax.broadcasted_iota(jnp.int32, (1, 1, 1, modes_all), 3)
    counted = jnp.sum((couplings[..., None] == columns).astype(jnp.float32), axis=2)
    row_ids = lax.broadcasted_iota(jnp.int32, (1, modes_all, modes_all), 1)
    col_ids = lax.broadcasted_iota(jnp.int32, (1, modes_all, modes_all), 2)
    off_diagonal = (row_ids != col_ids).astype(jnp.float32)
    return counted * weight * off_diagonal


def shards(solution, source, mean_conductivity, kl_fields, couplings, mode_index):
    modes_here = solution.shape[0]
    fields = kl_fields.shape[0]
    shape = solution.shape
    cells = shape[1] * shape[2] * shape[3]
    block_start = lax.axis_index("ma") * modes_here
    g_full = coupling_table(couplings, mode_index)
    stacked = jnp.concatenate([mean_conductivity[None], kl_fields], 0)
    padded_fields = extended(stacked, (("gx", 1),), 1)
    mean_pad = padded_fields[0]
    kl_pad = padded_fields[1:]
    padded_solution = extended(solution, (("gx", 1),), 1)
    image = solution + diffuse(mean_pad, padded_solution)
    terms = jnp.stack([diffuse(kl_pad[field_id], padded_solution) for field_id in range(fields)])
    terms = terms.reshape(fields, modes_here, cells)
    g_cols = lax.dynamic_slice_in_dim(g_full, block_start, modes_here, 2)
    coupled = lax.psum_scatter(
        jnp.einsum("kij,kjc->ic", g_cols, terms, precision=lax.Precision.HIGHEST),
        "ma",
        scatter_dimension=0,
        tiled=True,
    )
    image = image + coupled.reshape(shape)
    residual = source - image
    theta = 13.0
    delta = 12.0
    sigma = theta / delta
    rho = 1.0 / sigma
    direction = residual / theta
    correction = direction
    remain = residual
    for step in range(STEPS):
        padded_direction = extended(direction, (("gx", 1),), 1)
        applied = direction + diffuse(mean_pad, padded_direction)
        remain = remain - applied
        rho_next = 1.0 / (2.0 * sigma - rho)
        direction = rho_next * rho * direction + 2.0 * rho_next / delta * remain
        correction = correction + direction
        rho = rho_next
    return (residual, correction)


def solution(mesh):
    in_specs = (
        P("ma", "gx", None, None),
        P("ma", "gx", None, None),
        P("gx", None, None),
        P(None, "gx", None, None),
        P(),
        P(),
    )
    out_specs = (P("ma", "gx", None, None), P("ma", "gx", None, None))
    return jax.shard_map(shards, mesh=mesh, in_specs=in_specs, out_specs=out_specs, check_vma=False)
```

profile of v0, /device:TPU:0, one launch (start us, length us, event | category | flops | bytes accessed | tf_op | source)
XLA Modules:
  0.0 229.5 jit_solution(17499382940126329251)
XLA Ops:
  8.8 2.9 %collective-permute-start.2 = (f32[11,1,8,256]{3,2,1,0:T(8,128)}, f32[11,1,8,256]{3,2,1,0:T(8,128)}, u32[]{:S(2)}, u32[]{:S(2)}) collective-permute-start(f32[11,1,8,256]{3,2,1,0:T(8,128)} %pad_maximum_fusion), channel_id=1, source_target_pairs={{0,4},{4,8},{8,12},{12,16},{16,20},{20,24},{24,28},{28,0},{1,5},{5... | collective-permute-start | bytes 270344 | tf_op jit(solution)/shard_map/ppermute | solution.py:16
  11.7 3.0 %collective-permute-start = (f32[11,1,8,256]{3,2,1,0:T(8,128)}, f32[11,1,8,256]{3,2,1,0:T(8,128)}, u32[]{:S(2)}, u32[]{:S(2)}) collective-permute-start(f32[11,1,8,256]{3,2,1,0:T(8,128)} %pad_maximum_fusion), channel_id=1, source_target_pairs={{4,0},{8,4},{12,8},{16,12},{20,16},{24,20},{28,24},{0,28},{5,1},{9... | collective-permute-start | bytes 270344 | tf_op jit(solution)/shard_map/ppermute | solution.py:17
  14.7 2.0 collective-permute-start.1
  20.6 2.3 fusion.188
  24.8 2.4 %fusion.186 = (f32[64,1,8,255]{3,2,1,0:T(8,128)}, f32[64,1,8,255]{3,2,1,0:T(8,128)}) fusion(f32[64,1,8,256]{3,2,1,0:T(8,128)} %param.6), kind=kLoop, calls=%fused_computation.396 | loop fusion | bytes 2088960 | tf_op jit(solution)/shard_map/jit(_roll_static)/slice | solution.py:30
  31.9 2.5 %copy.80 = f32[10,256,64]{1,2,0:T(8,128)} copy(f32[10,256,64]{2,1,0:T(8,128)} %constant_dynamic-slice_fusion) | data formatting | bytes 1310720
  46.9 3.4 %multiply_add_fusion.2 = (f32[64,1,8,256]{3,2,1,0:T(8,128)}, f32[64,1,8,256]{3,2,1,0:T(8,128)S(1)}, f32[64,1,8,256]{3,2,1,0:T(8,128)S(1)}, f32[64,1,8,256]{3,2,1...) fusion(f32[8,256]{1,0:T(8,128)S(1)} %get-tuple-element.127, ...), kind=kLoop, calls=%fused_computation.60 | loop fusion | flops 2752512 | bytes 7389184 | tf_op jit(solution)/shard_map/add | solution.py:29
  56.0 2.4 %multiply_add_fusion.9 = (f32[64,1,8,256]{3,2,1,0:T(8,128)}, f32[64,1,8,256]{3,2,1,0:T(8,128)}) fusion(f32[64,1,8,256]{3,2,1,0:T(8,128)} %copy-done.1, f32[64,1,8,256]{3,2,1,0:T(8,128)S(1)} %get-tuple-element.13, f32[64,1,8,256]{3,2,1,0:T(8,128)S(1)} %get-tuple-element.12, f32[64,1,8,256]{3,2,1,0:T(8,128)S(1)} %get-tuple-element.11, ...), kind=kLoop, calls=%fused_computation.67 | loop fusion | flops 2883584 | bytes 4292608 | tf_op jit(solution)/shard_map/add | solution.py:29
  58.5 2.1 stack.34
  62.6 2.4 %multiply_add_fusion.7 = (f32[64,1,8,256]{3,2,1,0:T(8,128)}, f32[64,1,8,256]{3,2,1,0:T(8,128)}) fusion(f32[64,1,8,256]{3,2,1,0:T(8,128)} %copy-done.1, f32[64,1,8,256]{3,2,1,0:T(8,128)S(1)} %get-tuple-element.13, f32[64,1,8,256]{3,2,1,0:T(8,128)S(1)} %get-tuple-element.12, f32[64,1,8,256]{3,2,1,0:T(8,128)S(1)} %get-tuple-element.11, ...), kind=kLoop, calls=%fused_computation.65 | loop fusion | flops 2883584 | bytes 4292608 | tf_op jit(solution)/shard_map/add | solution.py:29
  69.0 2.4 %multiply_add_fusion.5 = (f32[64,1,8,256]{3,2,1,0:T(8,128)}, f32[64,1,8,256]{3,2,1,0:T(8,128)}) fusion(f32[64,1,8,256]{3,2,1,0:T(8,128)} %copy-done.1, f32[64,1,8,256]{3,2,1,0:T(8,128)S(1)} %get-tuple-element.13, f32[64,1,8,256]{3,2,1,0:T(8,128)S(1)} %get-tuple-element.12, f32[64,1,8,256]{3,2,1,0:T(8,128)S(1)} %get-tuple-element.11, ...), kind=kLoop, calls=%fused_computation.63 | loop fusion | flops 2883584 | bytes 4292608 | tf_op jit(solution)/shard_map/add | solution.py:29
  75.4 2.4 %multiply_add_fusion.3 = (f32[64,1,8,256]{3,2,1,0:T(8,128)}, f32[64,1,8,256]{3,2,1,0:T(8,128)}) fusion(f32[64,1,8,256]{3,2,1,0:T(8,128)} %copy-done.1, f32[64,1,8,256]{3,2,1,0:T(8,128)S(1)} %get-tuple-element.13, f32[64,1,8,256]{3,2,1,0:T(8,128)S(1)} %get-tuple-element.12, f32[64,1,8,256]{3,2,1,0:T(8,128)S(1)} %get-tuple-element.11, ...), kind=kLoop, calls=%fused_computation.61 | loop fusion | flops 2883584 | bytes 4292608 | tf_op jit(solution)/shard_map/add | solution.py:29
  83.6 2.0 constant_dynamic-update-slice_fusion.8
  96.4 8.8 %convolution_bitcast_fusion = f32[256,2048]{1,0:T(8,128)} fusion(f32[10,64,2048]{2,1,0:T(8,128)} %constant_dynamic-update-slice_fusion, f32[10,256,64]{1,2,0:T(8,128)S(1)} %copy-done.8, f32[256,64]{0,1:T(8,128)S(1)} %copy-done.10, f32[10,64]{1,0:T(8,128)S(1)} %copy-done.48, f32[10,256]{1,0:T(8,128)S(1)} %convert_bitcast_fusion), kind=kOutput, calls=%fused_computation.2 | convolution fusion | flops 4027023360 | bytes 8073728 | tf_op jit(solution)/shard_map/kij,kjc->ic/dot_general | solution.py:64
  105.5 32.8 %reduce-scatter.2.cloned.1.call-done = f32[64,2048]{1,0:T(8,128)} async-done(((f32[256,2048]{1,0:T(8,128)}), f32[64,2048]{1,0:T(8,128)}) %reduce-scatter.2.cloned.1.call-update) | async-done | bytes 524304 | tf_op jit(solution)/shard_map/reduce_scatter | solution.py:63
  142.8 3.2 %collective-permute-start.4 = (f32[64,1,8,256]{3,2,1,0:T(8,128)S(1)}, f32[64,1,8,256]{3,2,1,0:T(8,128)S(1)}, u32[]{:S(2)}, u32[]{:S(2)}) collective-permute-start(f32[64,1,8,256]{3,2,1,0:T(8,128)S(1)} %get-tuple-element.6), channel_id=1, source_target_pairs={{4,0},{8,4},{12,8},{16,12},{20,16},{24,20},{28,24},{0,28},{5,1},{9... | collective-permute-start | bytes 1572872 | tf_op jit(solution)/shard_map/ppermute | solution.py:17
  146.4 18.9 %collective-permute-done.5 = f32[64,1,8,256]{3,2,1,0:T(8,128)S(1)} collective-permute-done((f32[64,1,8,256]{3,2,1,0:T(8,128)S(1)}, f32[64,1,8,256]{3,2,1,0:T(8,128)S(1)}, u32[]{:S(2)}, u32[]{:S(2)}) %collective-permute-start.5) | collective-permute-done | bytes 524320 | tf_op jit(solution)/shard_map/ppermute | solution.py:16
  165.3 2.2 collective-permute-done.4
  168.7 4.4 %collective-permute-start.6 = (f32[64,1,8,256]{3,2,1,0:T(8,128)S(1)}, f32[64,1,8,256]{3,2,1,0:T(8,128)S(1)}, u32[]{:S(2)}, u32[]{:S(2)}) collective-permute-start(f32[64,1,8,256]{3,2,1,0:T(8,128)S(1)} %get-tuple-element.4), channel_id=1, source_target_pairs={{4,0},{8,4},{12,8},{16,12},{20,16},{24,20},{28,24},{0,28},{5,1},{9... | collective-permute-start | bytes 1572872 | tf_op jit(solution)/shard_map/ppermute | solution.py:17
  173.4 16.8 %collective-permute-done.7 = f32[64,1,8,256]{3,2,1,0:T(8,128)S(1)} collective-permute-done((f32[64,1,8,256]{3,2,1,0:T(8,128)S(1)}, f32[64,1,8,256]{3,2,1,0:T(8,128)S(1)}, u32[]{:S(2)}, u32[]{:S(2)}) %collective-permute-start.7) | collective-permute-done | bytes 524320 | tf_op jit(solution)/shard_map/ppermute | solution.py:16
  190.3 3.9 %collective-permute-done.6 = f32[64,1,8,256]{3,2,1,0:T(8,128)S(1)} collective-permute-done((f32[64,1,8,256]{3,2,1,0:T(8,128)S(1)}, f32[64,1,8,256]{3,2,1,0:T(8,128)S(1)}, u32[]{:S(2)}, u32[]{:S(2)}) %collective-permute-start.6) | collective-permute-done | bytes 524320 | tf_op jit(solution)/shard_map/ppermute | solution.py:17
  195.1 4.7 %collective-permute-start.8 = (f32[64,1,8,256]{3,2,1,0:T(8,128)S(1)}, f32[64,1,8,256]{3,2,1,0:T(8,128)S(1)}, u32[]{:S(2)}, u32[]{:S(2)}) collective-permute-start(f32[64,1,8,256]{3,2,1,0:T(8,128)S(1)} %get-tuple-element.2), channel_id=1, source_target_pairs={{4,0},{8,4},{12,8},{16,12},{20,16},{24,20},{28,24},{0,28},{5,1},{9... | collective-permute-start | bytes 1572872 | tf_op jit(solution)/shard_map/ppermute | solution.py:17
  200.1 17.2 %collective-permute-done.9 = f32[64,1,8,256]{3,2,1,0:T(8,128)S(1)} collective-permute-done((f32[64,1,8,256]{3,2,1,0:T(8,128)S(1)}, f32[64,1,8,256]{3,2,1,0:T(8,128)S(1)}, u32[]{:S(2)}, u32[]{:S(2)}) %collective-permute-start.9) | collective-permute-done | bytes 524320 | tf_op jit(solution)/shard_map/ppermute | solution.py:16
  217.3 3.8 %collective-permute-done.8 = f32[64,1,8,256]{3,2,1,0:T(8,128)S(1)} collective-permute-done((f32[64,1,8,256]{3,2,1,0:T(8,128)S(1)}, f32[64,1,8,256]{3,2,1,0:T(8,128)S(1)}, u32[]{:S(2)}, u32[]{:S(2)}) %collective-permute-start.8) | collective-permute-done | bytes 524320 | tf_op jit(solution)/shard_map/ppermute | solution.py:17
  (195 shorter events, 65.8 us)
Async XLA Ops:
  7.2 22.0 %copy-start.46 = (s32[10,256,2]{1,2,0:T(2,128)S(1)}, s32[10,256,2]{1,2,0:T(2,128)}, u32[]{:S(2)}) copy-start(s32[10,256,2]{1,2,0:T(2,128)} %param.10) | copy-start | bytes 61444
  7.2 131.2 %reduce-scatter.2.cloned.1.call-start = ((), (), s32[]{:S(2)}) async-start(), calls=%async_computation.1 | async-start | bytes 2621440 | tf_op jit(solution)/shard_map/reduce_scatter | solution.py:63
  8.8 27.8 %collective-permute-start.2 = (f32[11,1,8,256]{3,2,1,0:T(8,128)}, f32[11,1,8,256]{3,2,1,0:T(8,128)}, u32[]{:S(2)}, u32[]{:S(2)}) collective-permute-start(f32[11,1,8,256]{3,2,1,0:T(8,128)} %pad_maximum_fusion), channel_id=1, source_target_pairs={{0,4},{4,8},{8,12},{12,16},{16,20},{20,24},{24,28},{28,0},{1,5},{5... | collective-permute-start | bytes 270344 | tf_op jit(solution)/shard_map/ppermute | solution.py:16
  11.7 26.9 %collective-permute-start = (f32[11,1,8,256]{3,2,1,0:T(8,128)}, f32[11,1,8,256]{3,2,1,0:T(8,128)}, u32[]{:S(2)}, u32[]{:S(2)}) collective-permute-start(f32[11,1,8,256]{3,2,1,0:T(8,128)} %pad_maximum_fusion), channel_id=1, source_target_pairs={{4,0},{8,4},{12,8},{16,12},{20,16},{24,20},{28,24},{0,28},{5,1},{9... | collective-permute-start | bytes 270344 | tf_op jit(solution)/shard_map/ppermute | solution.py:17
  14.7 32.2 %collective-permute-start.1 = (f32[64,1,8,256]{3,2,1,0:T(8,128)}, f32[64,1,8,256]{3,2,1,0:T(8,128)}, u32[]{:S(2)}, u32[]{:S(2)}) collective-permute-start(f32[64,1,8,256]{3,2,1,0:T(8,128)} %param.6), channel_id=1, source_target_pairs={{4,0},{8,4},{12,8},{16,12},{20,16},{24,20},{28,24},{0,28},{5,1},{9... | collective-permute-start | bytes 1572872 | tf_op jit(solution)/shard_map/ppermute | solution.py:17
  16.8 30.1 %collective-permute-start.3 = (f32[64,1,8,256]{3,2,1,0:T(8,128)}, f32[64,1,8,256]{3,2,1,0:T(8,128)}, u32[]{:S(2)}, u32[]{:S(2)}) collective-permute-start(f32[64,1,8,256]{3,2,1,0:T(8,128)} %param.6), channel_id=1, source_target_pairs={{0,4},{4,8},{8,12},{12,16},{16,20},{20,24},{24,28},{28,0},{1,5},{5... | collective-permute-start | bytes 1572872 | tf_op jit(solution)/shard_map/ppermute | solution.py:16
  22.9 12.9 %copy-start.47 = (s32[256,10]{0,1:T(8,128)S(1)}, s32[256,10]{0,1:T(8,128)}, u32[]{:S(2)}) copy-start(s32[256,10]{0,1:T(8,128)} %param.11) | copy-start | bytes 30724
  22.9 13.6 %copy-start.3 = (f32[10,1,8,256]{3,2,1,0:T(8,128)S(1)}, f32[10,1,8,256]{3,2,1,0:T(8,128)}, u32[]{:S(2)}) copy-start(f32[10,1,8,256]{3,2,1,0:T(8,128)} %param.9) | copy-start | bytes 245764
  27.1 18.3 %copy-start.9 = (f32[1,8,256]{2,1,0:T(8,128)S(1)}, f32[1,8,256]{2,1,0:T(8,128)}, u32[]{:S(2)}) copy-start(f32[1,8,256]{2,1,0:T(8,128)} %param.8) | copy-start | bytes 24580
  27.1 19.7 %copy-start = (f32[64,1,8,256]{3,2,1,0:T(8,128)S(1)}, f32[64,1,8,256]{3,2,1,0:T(8,128)}, u32[]{:S(2)}) copy-start(f32[64,1,8,256]{3,2,1,0:T(8,128)} %param.6) | copy-start | bytes 1572868
  51.1 11.4 %copy-start.30 = (f32[8,256]{1,0:T(8,128)S(1)}, f32[8,256]{1,0:T(8,128)}, u32[]{:S(2)}) copy-start(f32[8,256]{1,0:T(8,128)} %get-tuple-element.110) | copy-start | bytes 24580
  51.1 11.4 %copy-start.31 = (f32[8,256]{1,0:T(8,128)S(1)}, f32[8,256]{1,0:T(8,128)}, u32[]{:S(2)}) copy-start(f32[8,256]{1,0:T(8,128)} %get-tuple-element.111) | copy-start | bytes 24580
  51.1 11.4 %copy-start.32 = (f32[8,256]{1,0:T(8,128)S(1)}, f32[8,256]{1,0:T(8,128)}, u32[]{:S(2)}) copy-start(f32[8,256]{1,0:T(8,128)} %get-tuple-element.112) | copy-start | bytes 24580
  81.6 14.8 %copy-start.10 = (f32[256,64]{0,1:T(8,128)S(1)}, f32[256,64]{0,1:T(8,128)}, u32[]{:S(2)}) copy-start(f32[256,64]{0,1:T(8,128)} %constant_dynamic-slice_fusion.2) | copy-start | bytes 196612
  81.6 14.8 %copy-start.48 = (f32[10,64]{1,0:T(8,128)S(1)}, f32[10,64]{1,0:T(8,128)}, u32[]{:S(2)}) copy-start(f32[10,64]{1,0:T(8,128)} %constant_dynamic-slice_fusion.1) | copy-start | bytes 7684
  83.6 12.0 %copy-start.7 = (f32[1,64,2048]{2,1,0:T(8,128)S(1)}, f32[1,64,2048]{2,1,0:T(8,128)}, u32[]{:S(2)}) copy-start(f32[1,64,2048]{2,1,0:T(8,128)} %stack.42) | copy-start | bytes 1572868
  83.6 12.9 %copy-start.8 = (f32[10,256,64]{1,2,0:T(8,128)S(1)}, f32[10,256,64]{1,2,0:T(8,128)}, u32[]{:S(2)}) copy-start(f32[10,256,64]{1,2,0:T(8,128)} %copy.80) | copy-start | bytes 1966084
  141.1 80.0 %copy-start.2 = (f32[64,1,8,256]{3,2,1,0:T(8,128)}, f32[64,1,8,256]{3,2,1,0:T(8,128)S(1)}, u32[]{:S(2)}) copy-start(f32[64,1,8,256]{3,2,1,0:T(8,128)S(1)} %get-tuple-element.7) | copy-start | bytes 1572868
  141.3 24.0 %collective-permute-start.5 = (f32[64,1,8,256]{3,2,1,0:T(8,128)S(1)}, f32[64,1,8,256]{3,2,1,0:T(8,128)S(1)}, u32[]{:S(2)}, u32[]{:S(2)}) collective-permute-start(f32[64,1,8,256]{3,2,1,0:T(8,128)S(1)} %get-tuple-element.6), channel_id=1, source_target_pairs={{0,4},{4,8},{8,12},{12,16},{16,20},{20,24},{24,28},{28,0},{1,5},{5... | collective-permute-start | bytes 1572872 | tf_op jit(solution)/shard_map/ppermute | solution.py:16
  142.8 24.6 %collective-permute-start.4 = (f32[64,1,8,256]{3,2,1,0:T(8,128)S(1)}, f32[64,1,8,256]{3,2,1,0:T(8,128)S(1)}, u32[]{:S(2)}, u32[]{:S(2)}) collective-permute-start(f32[64,1,8,256]{3,2,1,0:T(8,128)S(1)} %get-tuple-element.6), channel_id=1, source_target_pairs={{4,0},{8,4},{12,8},{16,12},{20,16},{24,20},{28,24},{0,28},{5,1},{9... | collective-permute-start | bytes 1572872 | tf_op jit(solution)/shard_map/ppermute | solution.py:17
  168.4 21.9 %collective-permute-start.7 = (f32[64,1,8,256]{3,2,1,0:T(8,128)S(1)}, f32[64,1,8,256]{3,2,1,0:T(8,128)S(1)}, u32[]{:S(2)}, u32[]{:S(2)}) collective-permute-start(f32[64,1,8,256]{3,2,1,0:T(8,128)S(1)} %get-tuple-element.4), channel_id=1, source_target_pairs={{0,4},{4,8},{8,12},{12,16},{16,20},{20,24},{24,28},{28,0},{1,5},{5... | collective-permute-start | bytes 1572872 | tf_op jit(solution)/shard_map/ppermute | solution.py:16
  168.7 25.4 %collective-permute-start.6 = (f32[64,1,8,256]{3,2,1,0:T(8,128)S(1)}, f32[64,1,8,256]{3,2,1,0:T(8,128)S(1)}, u32[]{:S(2)}, u32[]{:S(2)}) collective-permute-start(f32[64,1,8,256]{3,2,1,0:T(8,128)S(1)} %get-tuple-element.4), channel_id=1, source_target_pairs={{4,0},{8,4},{12,8},{16,12},{20,16},{24,20},{28,24},{0,28},{5,1},{9... | collective-permute-start | bytes 1572872 | tf_op jit(solution)/shard_map/ppermute | solution.py:17
  195.0 22.2 %collective-permute-start.9 = (f32[64,1,8,256]{3,2,1,0:T(8,128)S(1)}, f32[64,1,8,256]{3,2,1,0:T(8,128)S(1)}, u32[]{:S(2)}, u32[]{:S(2)}) collective-permute-start(f32[64,1,8,256]{3,2,1,0:T(8,128)S(1)} %get-tuple-element.2), channel_id=1, source_target_pairs={{0,4},{4,8},{8,12},{12,16},{16,20},{20,24},{24,28},{28,0},{1,5},{5... | collective-permute-start | bytes 1572872 | tf_op jit(solution)/shard_map/ppermute | solution.py:16
  195.1 26.0 %collective-permute-start.8 = (f32[64,1,8,256]{3,2,1,0:T(8,128)S(1)}, f32[64,1,8,256]{3,2,1,0:T(8,128)S(1)}, u32[]{:S(2)}, u32[]{:S(2)}) collective-permute-start(f32[64,1,8,256]{3,2,1,0:T(8,128)S(1)} %get-tuple-element.2), channel_id=1, source_target_pairs={{4,0},{8,4},{12,8},{16,12},{20,16},{24,20},{28,24},{0,28},{5,1},{9... | collective-permute-start | bytes 1572872 | tf_op jit(solution)/shard_map/ppermute | solution.py:17
  (36 other events, 339.4 us)
Sparse Core Ops, SparseCore 0:
  105.4 32.8 reduce-scatter.1
where the time goes:
time: 231 us; the launch traced here: 230 us
  waiting for transfers between devices  95.6 us (41%)
  local copies, waits for them, and re-layouts  56.7 us (25%)
  other arithmetic  31.4 us (14%)
  starting transfers between devices  22.4 us (10%)
  between operations  14.6 us (6%)
  matrix products  8.83 us (4%)
    ppermute x5, waiting for transfers between devices, extended(): before = lax.ppermute(last, axis, up)  52.9 us
    reduce_scatter x1, waiting for transfers between devices, shards(): lax.psum_scatter(jnp.einsum('kij,kjc->ic', g_cols, terms, precision=lax.P...  32.8 us
    another operation x11, local copies, waits for them, and re-layouts, shards(): jnp.stack([diffuse(kl_pad[field_id], padded_solution) for field_id in ran...  20.3 us
    unnamed x109, local copies, waits for them, and re-layouts  18.6 us
    ppermute x5, starting transfers between devices, extended(): after = lax.ppermute(initial, axis, down)  17.5 us
    add x6, other arithmetic, diffuse(): total + 0.5 * (center + jnp.roll(center, offset, which_dim)) * (values -...  14 us
    slice x16, local copies, waits for them, and re-layouts, diffuse(): jnp.roll(values, offset, which_dim)  9.92 us
    ppermute x5, waiting for transfers between devices, extended(): after = lax.ppermute(initial, axis, down)  9.87 us
  transfers between devices with their start and end apart: 11, of which 7 were waited for; matrix products, arithmetic and copies ran while one was open for 14% of the time, Pallas kernels for 0%

commit v1 on v0

v1 whole, which is shorter than its diff:
```python
import functools

import jax
import jax.numpy as jnp
from jax import lax
from jax.experimental import pallas as pl
from jax.experimental.pallas import tpu as pltpu
from jax.sharding import PartitionSpec as P

STEPS = 3
MESH = pl.DeviceIdType.MESH
VMEM = pl.BlockSpec(memory_space=pltpu.VMEM)
SMEM = pl.BlockSpec(memory_space=pltpu.SMEM)
LIMIT = 40 * 1024 * 1024


def greet(gx, n_gx, ma, n_ma):
    barrier = pltpu.get_barrier_semaphore()
    for d in range(1, n_gx):
        pl.semaphore_signal(barrier, inc=1, device_id={"gx": lax.rem(gx + d, n_gx)}, device_id_type=MESH)
    for d in range(1, n_ma):
        pl.semaphore_signal(barrier, inc=1, device_id={"ma": lax.rem(ma + d, n_ma)}, device_id_type=MESH)
    pl.semaphore_wait(barrier, max(n_gx - 1, 0) + max(n_ma - 1, 0))


def remote(src, dst, send, recv, axis, index):
    copy = pltpu.make_async_remote_copy(
        src_ref=src, dst_ref=dst, send_sem=send, recv_sem=recv, device_id={axis: index}, device_id_type=MESH
    )
    copy.start()
    return copy


def gather_kernel(n_gx, n_ma, v_ref, c_ref, all_ref, side_ref, mean_ref, s_v, r_v, s_c, r_c, s_m, r_m):
    gx, ma = lax.axis_index("gx"), lax.axis_index("ma")
    modes = v_ref.shape[0]
    greet(gx, n_gx, ma, n_ma)
    mine = pl.ds(ma * modes, modes)
    copies = []
    for d in range(n_ma - 1, 0, -1):
        copies.append(
            remote(v_ref, all_ref.at[mine], s_v.at[d], r_v.at[d], "ma", lax.rem(ma + d, n_ma))
        )
    copies.append(remote(c_ref, side_ref.at[1], s_c.at[1], r_c.at[1], "gx", lax.rem(gx + 1, n_gx)))
    copies.append(remote(c_ref, side_ref.at[0], s_c.at[0], r_c.at[0], "gx", lax.rem(gx + n_gx - 1, n_gx)))
    for d in range(1, n_gx):
        copies.append(
            remote(c_ref.at[0], mean_ref.at[gx], s_m.at[d], r_m.at[d], "gx", lax.rem(gx + d, n_gx))
        )
    all_ref[mine] = v_ref[...]
    mean_ref[gx] = c_ref[0]
    for copy in copies:
        copy.wait()


def faces_of(c):
    ny, nz = c.shape[-2], c.shape[-1]
    return [
        0.5 * (c + pltpu.roll(c, ny - 1, c.ndim - 2)),
        0.5 * (c + pltpu.roll(c, 1, c.ndim - 2)),
        0.5 * (c + pltpu.roll(c, nz - 1, c.ndim - 1)),
        0.5 * (c + pltpu.roll(c, 1, c.ndim - 1)),
    ]


def shift_faces(q):
    ny, nz = q[0].shape[-2], q[0].shape[-1]
    d = q[0].ndim
    return (
        pltpu.roll(q[1], ny - 1, d - 2)
        + pltpu.roll(q[0], 1, d - 2)
        + pltpu.roll(q[3], nz - 1, d - 1)
        + pltpu.roll(q[2], 1, d - 1)
    )


def couple_kernel(group, start_ref, part_ref, wt_ref, all_ref, src_ref, c_ref, side_ref, u_ref, qr_ref, ql_ref, f_ref):
    fields = c_ref.shape[0]
    modes = src_ref.shape[0]
    start = start_ref[0]
    for k in range(fields):
        c = c_ref[k]
        for m, face in enumerate(faces_of(c)):
            f_ref[m, k] = face
        f_ref[4, k] = 0.5 * (c + side_ref[0, k])
        f_ref[5, k] = 0.5 * (c + side_ref[1, k])

    def body(step, carry):
        base = step * group
        values = [all_ref[start + base + g] for g in range(group)]
        f = [f_ref[m, 0] for m in range(6)]
        q = [[f[m] * values[g] for m in range(6)] for g in range(group)]
        for k in range(1, fields):
            row = 2 * (k - 1)
            f = [f_ref[m, k] for m in range(6)]
            for g in range(group):
                i = base + g
                h = wt_ref[row, i] * all_ref[part_ref[row, i]] + wt_ref[row + 1, i] * all_ref[part_ref[row + 1, i]]
                q[g] = [q[g][m] + f[m] * h for m in range(6)]
        for g in range(group):
            total = q[g][0] + q[g][1] + q[g][2] + q[g][3] + q[g][4] + q[g][5]
            image = values[g] + total - shift_faces(q[g])
            u_ref[base + g] = src_ref[base + g] - image
            qr_ref[base + g] = q[g][4]
            ql_ref[base + g] = q[g][5]
        return carry

    lax.fori_loop(0, modes // group, body, 0)


def chebyshev_kernel(
    n_gx, u_ref, qr_ref, ql_ref, mean_ref, res_ref, cor_ref,
    from_left, from_right, trans, back, f_ref, s_r, r_r, s_l, r_l, s_t, r_t, s_b, r_b,
):
    gx = lax.axis_index("gx")
    modes = u_ref.shape[0]
    part = modes // n_gx
    right, left = lax.rem(gx + 1, n_gx), lax.rem(gx + n_gx - 1, n_gx)
    greet(gx, n_gx, 0, 1)
    order = list(range(1, n_gx)) + [0]
    halos = []
    for d in order:
        rows = pl.ds(d * part, part)
        halos.append(
            (
                remote(qr_ref.at[rows], from_left.at[rows], s_r.at[d], r_r.at[d], "gx", right),
                remote(ql_ref.at[rows], from_right.at[rows], s_l.at[d], r_l.at[d], "gx", left),
            )
        )
    for s in range(n_gx):
        c = mean_ref[s]
        after = mean_ref[(s + 1) % n_gx]
        before = mean_ref[(s + n_gx - 1) % n_gx]
        f = faces_of(c) + [0.5 * (c + after), 0.5 * (c + before)]
        for m in range(6):
            f_ref[m, s] = f[m]
        f_ref[6, s] = f[0] + f[1] + f[2] + f[3] + f[4] + f[5] + 1.0
    sent = []
    for d, pair in zip(order, halos):
        rows = pl.ds(d * part, part)
        pair[0].wait()
        pair[1].wait()
        res_ref[rows] = u_ref[rows] + from_left[rows] + from_right[rows]
    for d in range(n_gx):
        target = lax.rem(gx + d, n_gx)
        rows = pl.ds(target * part, part)
        if d == 0:
            trans[gx] = res_ref[rows]
        else:
            sent.append(
                remote(res_ref.at[rows], trans.at[gx], s_t.at[d], r_t.at[d], "gx", target)
            )
    for copy in sent:
        copy.wait()

    theta = 13.0
    delta = 12.0
    sigma = theta / delta

    def one(mode, carry):
        remain = [trans[s, mode] for s in range(n_gx)]
        direction = [r * (1.0 / theta) for r in remain]
        total = direction
        rho = 1.0 / sigma
        for _ in range(STEPS):
            rho_next = 1.0 / (2.0 * sigma - rho)
            ny, nz = direction[0].shape
            fresh = []
            for s in range(n_gx):
                v = direction[s]
                applied = (
                    f_ref[6, s] * v
                    - f_ref[0, s] * pltpu.roll(v, ny - 1, 0)
                    - f_ref[1, s] * pltpu.roll(v, 1, 0)
                    - f_ref[2, s] * pltpu.roll(v, nz - 1, 1)
                    - f_ref[3, s] * pltpu.roll(v, 1, 1)
                    - f_ref[4, s] * direction[(s + 1) % n_gx]
                    - f_ref[5, s] * direction[(s + n_gx - 1) % n_gx]
                )
                fresh.append(remain[s] - applied)
            remain = fresh
            direction = [
                (rho_next * rho) * direction[s] + (2.0 * rho_next / delta) * remain[s] for s in range(n_gx)
            ]
            total = [total[s] + direction[s] for s in range(n_gx)]
            rho = rho_next
        for s in range(n_gx):
            back[s, mode] = total[s]
        return carry

    lax.fori_loop(0, part, one, 0)
    sent = []
    for d in range(n_gx):
        target = lax.rem(gx + d, n_gx)
        rows = pl.ds(gx * part, part)
        if d == 0:
            cor_ref[rows] = back[gx]
        else:
            sent.append(
                remote(back.at[target], cor_ref.at[rows], s_b.at[d], r_b.at[d], "gx", target)
            )
    for copy in sent:
        copy.wait()


def shards(n_gx, n_ma, solution, source, mean_conductivity, kl_fields, couplings, mode_index):
    modes = solution.shape[0]
    shape = solution.shape
    ny, nz = shape[2], shape[3]
    fields = kl_fields.shape[0]
    start = lax.axis_index("ma") * modes
    f32 = jnp.float32
    here = lax.dynamic_slice_in_dim(couplings, start, modes, 1)
    degree = lax.dynamic_slice_in_dim(mode_index, start, modes, 0).T.astype(f32)
    ids = start + lax.broadcasted_iota(jnp.int32, (1, modes, 1), 1)
    strength = jnp.sqrt(jnp.stack([degree + 1.0, degree], -1))
    weight = jnp.where(here != ids, strength, 0.0)
    partner = here.transpose(0, 2, 1).reshape(2 * fields, modes)
    weight = weight.transpose(0, 2, 1).reshape(2 * fields, modes)
    stacked = jnp.concatenate([mean_conductivity, kl_fields[:, 0]], 0)
    v = solution.reshape(modes, ny, nz)
    src = source.reshape(modes, ny, nz)
    dma = pltpu.SemaphoreType.DMA
    everything, sides, means = pl.pallas_call(
        functools.partial(gather_kernel, n_gx, n_ma),
        out_shape=(
            jax.ShapeDtypeStruct((n_ma * modes, ny, nz), f32),
            jax.ShapeDtypeStruct((2, fields + 1, ny, nz), f32),
            jax.ShapeDtypeStruct((n_gx, ny, nz), f32),
        ),
        in_specs=[VMEM] * 2,
        out_specs=(VMEM,) * 3,
        scratch_shapes=[dma((n_ma,)), dma((n_ma,)), dma((2,)), dma((2,)), dma((n_gx,)), dma((n_gx,))],
        compiler_params=pltpu.CompilerParams(collective_id=0, has_side_effects=True, vmem_limit_bytes=LIMIT),
    )(v, stacked)
    field = jax.ShapeDtypeStruct((modes, ny, nz), f32)
    group = 2 if modes % 2 == 0 else 1
    u, qr, ql = pl.pallas_call(
        functools.partial(couple_kernel, group),
        out_shape=(field,) * 3,
        in_specs=[SMEM] * 3 + [VMEM] * 4,
        out_specs=(VMEM,) * 3,
        scratch_shapes=[pltpu.VMEM((6, fields + 1, ny, nz), f32)],
        compiler_params=pltpu.CompilerParams(vmem_limit_bytes=LIMIT),
    )(start.reshape(1).astype(jnp.int32), partner, weight, everything, src, stacked, sides)
    part = modes // n_gx
    residual, correction = pl.pallas_call(
        functools.partial(chebyshev_kernel, n_gx),
        out_shape=(field,) * 2,
        in_specs=[VMEM] * 4,
        out_specs=(VMEM,) * 2,
        scratch_shapes=[
            pltpu.VMEM((modes, ny, nz), f32),
            pltpu.VMEM((modes, ny, nz), f32),
            pltpu.VMEM((n_gx, part, ny, nz), f32),
            pltpu.VMEM((n_gx, part, ny, nz), f32),
            pltpu.VMEM((7, n_gx, ny, nz), f32),
        ]
        + [dma((n_gx,))] * 8,
        compiler_params=pltpu.CompilerParams(collective_id=1, has_side_effects=True, vmem_limit_bytes=LIMIT),
    )(u, qr, ql, means)
    return residual.reshape(shape), correction.reshape(shape)


def solution(mesh):
    in_specs = (
        P("ma", "gx", None, None),
        P("ma", "gx", None, None),
        P("gx", None, None),
        P(None, "gx", None, None),
        P(),
        P(),
    )
    out_specs = (P("ma", "gx", None, None), P("ma", "gx", None, None))
    body = functools.partial(shards, mesh.shape["gx"], mesh.shape["ma"])
    return jax.shard_map(body, mesh=mesh, in_specs=in_specs, out_specs=out_specs, check_vma=False)
```

time: 231 us -> 92.6 us (0.40)
  the two profiles are of different devices: /device:TPU:0 before, /device:TPU:28 now
where the time goes in v1:
time: 92.6 us; the launch traced here: 92.3 us
  Pallas kernels  85.3 us (92%)
  local copies, waits for them, and re-layouts  3.79 us (4%)
  other arithmetic  2.47 us (3%)
    pallas_call x1, Pallas kernels, shards(): pl.pallas_call(functools.partial(chebyshev_kernel, n_gx), out_shape=(fiel...  53.7 us
    pallas_call x1, Pallas kernels, shards(): pl.pallas_call(functools.partial(gather_kernel, n_gx, n_ma), out_shape=(j...  25.8 us
    pallas_call x1, Pallas kernels, shards(): pl.pallas_call(functools.partial(couple_kernel, group), out_shape=(field,...  5.82 us
    unnamed x9, local copies, waits for them, and re-layouts  3.67 us

profile of v1, /device:TPU:28, one launch (start us, length us, event | category | flops | bytes accessed | tf_op | source)
XLA Modules:
  0.0 92.3 jit_solution(4369841676037584881)
XLA Ops:
  0.6 0.0 copy-start
  0.7 0.8 convert_bitcast_fusion
  1.4 0.8 fusion.2
  2.2 0.0 copy-done
  2.2 0.1 constant_dynamic-slice_fusion
  2.4 0.9 pad_maximum_fusion.c_ref
  3.3 0.0 copy-start.2
  3.3 1.0 %copy-done.2 = f32[64,1,8,256]{3,2,1,0:T(8,128)S(1)} copy-done((f32[64,1,8,256]{3,2,1,0:T(8,128)S(1)}, f32[64,1,8,256]{3,2,1,0:T(8,128)}, u32[]{:S(2)}) %copy-start.2) | copy-done | bytes 524312
  4.3 25.8 %shard_map.77 = (f32[256,8,256]{2,1,0:T(8,128)S(1)}, f32[2,11,8,256]{3,2,1,0:T(8,128)S(1)}, f32[8,8,256]{2,1,0:T(8,128)S(1)}) custom-call(f32[64,8,256]{2,1,0:T(8,128)S(1)} %bitcast.25, f32[11,8,256]{2,1,0:T(8,128)S(1)} %pad_maximum_fusion.c_ref), custom_call_target="tpu_custom_call" | custom-call | tf_op jit(solution)/shard_map/pallas_call | solution.py:224
  30.1 0.0 copy-start.1
  30.1 1.0 %copy-done.1 = f32[64,1,8,256]{3,2,1,0:T(8,128)S(1)} copy-done((f32[64,1,8,256]{3,2,1,0:T(8,128)S(1)}, f32[64,1,8,256]{3,2,1,0:T(8,128)}, u32[]{:S(2)}) %copy-start.1) | copy-done | bytes 524312
  31.2 5.8 %shard_map.78 = (f32[64,8,256]{2,1,0:T(8,128)S(1)}, f32[64,8,256]{2,1,0:T(8,128)S(1)}, f32[64,8,256]{2,1,0:T(8,128)S(1)}) custom-call(s32[1]{0:T(128)} %bitcast.start_ref, s32[20,64]{1,0:T(8,128)S(1)} %reshape.31.part_ref, f32[20,64]{1,0:T(8,128)S(1)} %reshape.32.wt_ref, f32[256,8,256]{2,1,0:T(8,128)S(1)} %get-tuple-element.10.all_ref, ...), custom_call_target="tpu_custom_call" | custom-call | tf_op jit(solution)/shard_map/pallas_call | solution.py:238
  37.0 53.7 %shard_map.79 = (f32[64,8,256]{2,1,0:T(8,128)S(1)}, f32[64,8,256]{2,1,0:T(8,128)S(1)}) custom-call(f32[64,8,256]{2,1,0:T(8,128)S(1)} %get-tuple-element.12.u_ref, f32[64,8,256]{2,1,0:T(8,128)S(1)} %get-tuple-element.13.qr_ref, f32[64,8,256]{2,1,0:T(8,128)S(1)} %get-tuple-element.14.ql_ref, f32[8,8,256]{2,1,0:T(8,128)S(1)} %get-tuple-element.15.mean_ref), custom_call_target="tpu_custom_call" | custom-call | tf_op jit(solution)/shard_map/pallas_call | solution.py:247
  90.7 0.8 copy.21
  91.5 0.8 copy.22
  (7 shorter events, 0.1 us)
Async XLA Ops:
  0.6 1.6 %copy-start = (s32[10,256,2]{1,2,0:T(2,128)S(1)}, s32[10,256,2]{1,2,0:T(2,128)}, u32[]{:S(2)}) copy-start(s32[10,256,2]{1,2,0:T(2,128)} %param.10) | copy-start | bytes 61444
  3.3 1.0 %copy-start.2 = (f32[64,1,8,256]{3,2,1,0:T(8,128)S(1)}, f32[64,1,8,256]{3,2,1,0:T(8,128)}, u32[]{:S(2)}) copy-start(f32[64,1,8,256]{3,2,1,0:T(8,128)} %param.6) | copy-start | bytes 1572868
  30.1 1.0 %copy-start.1 = (f32[64,1,8,256]{3,2,1,0:T(8,128)S(1)}, f32[64,1,8,256]{3,2,1,0:T(8,128)}, u32[]{:S(2)}) copy-start(f32[64,1,8,256]{3,2,1,0:T(8,128)} %param.7) | copy-start | bytes 1572868

commit v2 on v0

v2 whole, which is shorter than its diff:
```python
import functools

import jax
import jax.numpy as jnp
from jax import lax
from jax.experimental import pallas as pl
from jax.experimental.pallas import tpu as pltpu
from jax.sharding import PartitionSpec as P

STEPS = 3
MESH = pl.DeviceIdType.MESH
VMEM = pl.BlockSpec(memory_space=pltpu.VMEM)
SMEM = pl.BlockSpec(memory_space=pltpu.SMEM)
LIMIT = 40 * 1024 * 1024


def greet(gx, n_gx, ma, n_ma):
    barrier = pltpu.get_barrier_semaphore()
    for d in range(1, n_gx):
        pl.semaphore_signal(barrier, inc=1, device_id={"gx": lax.rem(gx + d, n_gx)}, device_id_type=MESH)
    for d in range(1, n_ma):
        pl.semaphore_signal(barrier, inc=1, device_id={"ma": lax.rem(ma + d, n_ma)}, device_id_type=MESH)
    pl.semaphore_wait(barrier, max(n_gx - 1, 0) + max(n_ma - 1, 0))


def remote(src, dst, send, recv, axis, index):
    copy = pltpu.make_async_remote_copy(
        src_ref=src, dst_ref=dst, send_sem=send, recv_sem=recv, device_id={axis: index}, device_id_type=MESH
    )
    copy.start()
    return copy


def faces_of(c):
    ny, nz = c.shape[-2], c.shape[-1]
    return [
        0.5 * (c + pltpu.roll(c, ny - 1, c.ndim - 2)),
        0.5 * (c + pltpu.roll(c, 1, c.ndim - 2)),
        0.5 * (c + pltpu.roll(c, nz - 1, c.ndim - 1)),
        0.5 * (c + pltpu.roll(c, 1, c.ndim - 1)),
    ]


def shift_faces(q):
    ny, nz = q[0].shape[-2], q[0].shape[-1]
    d = q[0].ndim
    return (
        pltpu.roll(q[1], ny - 1, d - 2)
        + pltpu.roll(q[0], 1, d - 2)
        + pltpu.roll(q[3], nz - 1, d - 1)
        + pltpu.roll(q[2], 1, d - 1)
    )


def kernel(
    n_gx, n_ma, chunks, pieces, part_ref, wt_ref, v_ref, src_ref, c_ref, res_ref, cor_ref,
    all_ref, side_ref, mean_ref, f_ref, fm_ref, u_ref, qr_ref, ql_ref, from_left, from_right, trans, back,
    s_p, r_p, s_f, r_f, s_o, r_o, s_c, r_c, s_m, r_m, s_h, r_h, s_t, r_t, s_b, r_b,
):
    gx, ma = lax.axis_index("gx"), lax.axis_index("ma")
    right, left = lax.rem(gx + 1, n_gx), lax.rem(gx + n_gx - 1, n_gx)
    modes = v_ref.shape[0]
    fields = c_ref.shape[0]
    part = modes // n_gx
    sub = part // chunks
    pairs = n_ma // 2
    twin = ma + 1 - 2 * lax.rem(ma, 2)
    greet(gx, n_gx, ma, n_ma)

    size = modes // pieces
    far = {}
    for p in range(pieces):
        for d in range(1, pairs):
            far[p, d] = remote(
                v_ref.at[pl.ds(p * size, size)],
                all_ref.at[pl.ds(ma * modes + p * size, size)],
                s_p.at[p, d], r_p.at[p, d], "ma", lax.rem(ma + 2 * d, n_ma),
            )
    side = [
        remote(c_ref, side_ref.at[1], s_c.at[1], r_c.at[1], "gx", right),
        remote(c_ref, side_ref.at[0], s_c.at[0], r_c.at[0], "gx", left),
    ]
    near = [remote(v_ref, all_ref.at[pl.ds(ma * modes, modes)], s_o.at[0], r_o.at[0], "ma", twin)]
    means = [
        remote(c_ref.at[0], mean_ref.at[gx], s_m.at[d], r_m.at[d], "gx", lax.rem(gx + d, n_gx))
        for d in range(1, n_gx)
    ]
    all_ref[pl.ds(ma * modes, modes)] = v_ref[...]
    mean_ref[gx] = c_ref[0]
    for k in range(fields):
        for m, face in enumerate(faces_of(c_ref[k])):
            f_ref[m, k] = face
    for p in range(pieces):
        for d in range(1, pairs):
            far[p, d].wait()
            rows = pl.ds(lax.rem(ma + n_ma - 2 * d, n_ma) * modes + p * size, size)
            near.append(
                remote(all_ref.at[rows], all_ref.at[rows], s_f.at[p, d], r_f.at[p, d], "ma", twin)
            )
        if p == 0:
            for copy in side:
                copy.wait()
            for k in range(fields):
                f_ref[4, k] = 0.5 * (c_ref[k] + side_ref[0, k])
                f_ref[5, k] = 0.5 * (c_ref[k] + side_ref[1, k])
            for copy in means:
                copy.wait()
            for s in range(n_gx):
                c = mean_ref[s]
                f = faces_of(c) + [
                    0.5 * (c + mean_ref[(s + 1) % n_gx]),
                    0.5 * (c + mean_ref[(s + n_gx - 1) % n_gx]),
                ]
                for m in range(6):
                    fm_ref[m, s] = f[m]
                fm_ref[6, s] = f[0] + f[1] + f[2] + f[3] + f[4] + f[5] + 1.0
    for copy in near:
        copy.wait()

    halos = []
    for q in range(chunks):

        def body(d, carry):
            base = d * part + q * sub
            values = [v_ref[base + g] for g in range(sub)]
            f = [f_ref[m, 0] for m in range(6)]
            sums = [[f[m] * values[g] for m in range(6)] for g in range(sub)]
            for k in range(1, fields):
                row = 2 * (k - 1)
                f = [f_ref[m, k] for m in range(6)]
                for g in range(sub):
                    i = base + g
                    h = wt_ref[row, i] * all_ref[part_ref[row, i]] + wt_ref[row + 1, i] * all_ref[part_ref[row + 1, i]]
                    sums[g] = [sums[g][m] + f[m] * h for m in range(6)]
            for g in range(sub):
                t = sums[g]
                image = values[g] + (t[0] + t[1] + t[2] + t[3] + t[4] + t[5]) - shift_faces(t)
                u_ref[q, d, g] = src_ref[base + g] - image
                qr_ref[q, d, g] = t[4]
                ql_ref[q, d, g] = t[5]
            return carry

        lax.fori_loop(0, n_gx, body, 0)
        halos.append(
            (
                remote(qr_ref.at[q], from_left.at[q], s_h.at[q, 0], r_h.at[q, 0], "gx", right),
                remote(ql_ref.at[q], from_right.at[q], s_h.at[q, 1], r_h.at[q, 1], "gx", left),
            )
        )

    moved = {}
    returned = []

    def settle(q):
        for copy in halos[q]:
            copy.wait()
        cols = pl.ds(q * sub, sub)
        for d in range(n_gx):
            res_ref[d, cols] = u_ref[q, d] + from_left[q, d] + from_right[q, d]
        moved[q] = [
            remote(
                res_ref.at[lax.rem(gx + d, n_gx), cols], trans.at[q, gx],
                s_t.at[q, d], r_t.at[q, d], "gx", lax.rem(gx + d, n_gx),
            )
            for d in range(1, n_gx)
        ]
        trans[q, gx] = res_ref[gx, cols]

    def polish(q):
        for copy in moved[q]:
            copy.wait()
        theta = 13.0
        delta = 12.0
        sigma = theta / delta

        def one(mode, carry):
            remain = [trans[q, s, mode] for s in range(n_gx)]
            direction = [r * (1.0 / theta) for r in remain]
            total = direction
            rho = 1.0 / sigma
            for _ in range(STEPS):
                rho_next = 1.0 / (2.0 * sigma - rho)
                ny, nz = direction[0].shape
                fresh = []
                for s in range(n_gx):
                    v = direction[s]
                    applied = (
                        fm_ref[6, s] * v
                        - fm_ref[0, s] * pltpu.roll(v, ny - 1, 0)
                        - fm_ref[1, s] * pltpu.roll(v, 1, 0)
                        - fm_ref[2, s] * pltpu.roll(v, nz - 1, 1)
                        - fm_ref[3, s] * pltpu.roll(v, 1, 1)
                        - fm_ref[4, s] * direction[(s + 1) % n_gx]
                        - fm_ref[5, s] * direction[(s + n_gx - 1) % n_gx]
                    )
                    fresh.append(remain[s] - applied)
                remain = fresh
                direction = [
                    (rho_next * rho) * direction[s] + (2.0 * rho_next / delta) * remain[s] for s in range(n_gx)
                ]
                total = [total[s] + direction[s] for s in range(n_gx)]
                rho = rho_next
            for s in range(n_gx):
                back[q, s, mode] = total[s]
            return carry

        lax.fori_loop(0, sub, one, 0)
        cols = pl.ds(q * sub, sub)
        for d in range(1, n_gx):
            target = lax.rem(gx + d, n_gx)
            returned.append(
                remote(back.at[q, target], cor_ref.at[gx, cols], s_b.at[q, d], r_b.at[q, d], "gx", target)
            )
        cor_ref[gx, cols] = back[q, gx]

    settle(0)
    for q in range(chunks):
        if q + 1 < chunks:
            settle(q + 1)
        polish(q)
    for copy in returned:
        copy.wait()


def shards(n_gx, n_ma, solution, source, mean_conductivity, kl_fields, couplings, mode_index):
    modes = solution.shape[0]
    shape = solution.shape
    ny, nz = shape[2], shape[3]
    fields = kl_fields.shape[0]
    start = lax.axis_index("ma") * modes
    f32 = jnp.float32
    here = lax.dynamic_slice_in_dim(couplings, start, modes, 1)
    degree = lax.dynamic_slice_in_dim(mode_index, start, modes, 0).T.astype(f32)
    ids = start + lax.broadcasted_iota(jnp.int32, (1, modes, 1), 1)
    strength = jnp.sqrt(jnp.stack([degree + 1.0, degree], -1))
    weight = jnp.where(here != ids, strength, 0.0)
    partner = here.transpose(0, 2, 1).reshape(2 * fields, modes)
    weight = weight.transpose(0, 2, 1).reshape(2 * fields, modes)
    stacked = jnp.concatenate([mean_conductivity, kl_fields[:, 0]], 0)
    v = solution.reshape(modes, ny, nz)
    src = source.reshape(modes, ny, nz)
    part = modes // n_gx
    chunks = next(n for n in (4, 2, 1) if part % n == 0)
    pieces = next(n for n in (4, 2, 1) if modes % n == 0)
    sub = part // chunks
    pairs = n_ma // 2
    dma = pltpu.SemaphoreType.DMA
    vmem = lambda *lead: pltpu.VMEM(lead + (ny, nz), f32)
    field = jax.ShapeDtypeStruct((n_gx, part, ny, nz), f32)
    residual, correction = pl.pallas_call(
        functools.partial(kernel, n_gx, n_ma, chunks, pieces),
        out_shape=(field,) * 2,
        in_specs=[SMEM] * 2 + [VMEM] * 3,
        out_specs=(VMEM,) * 2,
        scratch_shapes=[
            vmem(n_ma * modes),
            vmem(2, fields + 1),
            vmem(n_gx),
            vmem(6, fields + 1),
            vmem(7, n_gx),
        ]
        + [vmem(chunks, n_gx, sub)] * 7
        + [dma((pieces, pairs))] * 4
        + [dma((1,))] * 2
        + [dma((2,))] * 2
        + [dma((n_gx,))] * 2
        + [dma((chunks, 2))] * 2
        + [dma((chunks, n_gx))] * 4,
        compiler_params=pltpu.CompilerParams(collective_id=0, has_side_effects=True, vmem_limit_bytes=LIMIT),
    )(partner, weight, v, src, stacked)
    return residual.reshape(shape), correction.reshape(shape)


def solution(mesh):
    in_specs = (
        P("ma", "gx", None, None),
        P("ma", "gx", None, None),
        P("gx", None, None),
        P(None, "gx", None, None),
        P(),
        P(),
    )
    out_specs = (P("ma", "gx", None, None), P("ma", "gx", None, None))
    body = functools.partial(shards, mesh.shape["gx"], mesh.shape["ma"])
    return jax.shard_map(body, mesh=mesh, in_specs=in_specs, out_specs=out_specs, check_vma=False)
```

time: 231 us -> 78.4 us (0.34)
  waiting for transfers between devices: 95.6 us -> 0 us
  Pallas kernels: 0 us -> 71.9 us
  local copies, waits for them, and re-layouts: 56.7 us -> 5.28 us
  other arithmetic: 31.4 us -> 0.18 us
  starting transfers between devices: 22.4 us -> 0 us
  between operations: 14.6 us -> 0.73 us
  matrix products: 8.83 us -> 0 us
    pallas_call x0 -> x1, Pallas kernels: none -> 71.9 us  [shards(): pl.pallas_call(functools.partial(kernel, n_gx, n_ma, chunks, pieces), out...]
    ppermute x10 -> x0, waiting for transfers between devices: 62.8 us -> none  [the longest x5 52.9 us: extended(): before = lax.ppermute(last, axis, up)]
    reduce_scatter x1 -> x0, waiting for transfers between devices: 32.8 us -> none  [shards(): lax.psum_scatter(jnp.einsum('kij,kjc->ic', g_cols, terms, precision=lax.P...]
    ppermute x10 -> x0, starting transfers between devices: 22.3 us -> none  [the longest x5 17.5 us: extended(): after = lax.ppermute(initial, axis, down)]
    another operation x11 -> x0, local copies, waits for them, and re-layouts: 20.3 us -> none  [shards(): jnp.stack([diffuse(kl_pad[field_id], padded_solution) for field_id in ran...]
    add x9 -> x1, other arithmetic: 17 us -> 0.01 us  [shards(): ids = start + lax.broadcasted_iota(jnp.int32, (1, modes, 1), 1)]
    unnamed x109 -> x15, local copies, waits for them, and re-layouts: 18.6 us -> 5.17 us
    slice x17 -> x0, local copies, waits for them, and re-layouts: 10.6 us -> none  [the longest x16 9.92 us: diffuse(): jnp.roll(values, offset, which_dim)]
  transfers between devices with their start and end apart: 11 -> 0, of which waited for: 7 -> 0; matrix products, arithmetic and copies ran while one was open for 14% -> 0% of each run, Pallas kernels for 0% -> 0%
where the time goes in v2:
time: 78.4 us; the launch traced here: 78 us
  Pallas kernels  71.9 us (92%)
  local copies, waits for them, and re-layouts  5.28 us (7%)
    pallas_call x1, Pallas kernels, shards(): pl.pallas_call(functools.partial(kernel, n_gx, n_ma, chunks, pieces), out...  71.9 us
    unnamed x15, local copies, waits for them, and re-layouts  5.17 us

profile of v2, /device:TPU:0, one launch (start us, length us, event | category | flops | bytes accessed | tf_op | source)
XLA Modules:
  0.0 78.0 jit_solution(17451828063514491737)
XLA Ops:
  0.6 0.0 copy-start
  0.6 0.0 copy-start.4
  0.7 0.7 copy-done.4
  1.4 0.1 convert_bitcast_fusion
  1.4 0.1 fusion.2
  1.5 0.0 copy-done
  1.5 0.1 constant_dynamic-slice_fusion
  1.6 0.0 copy-start.3
  1.7 0.0 copy-start.5
  1.7 0.8 %copy-done.3 = f32[10,1,8,256]{3,2,1,0:T(8,128)S(1)} copy-done((f32[10,1,8,256]{3,2,1,0:T(8,128)S(1)}, f32[10,1,8,256]{3,2,1,0:T(8,128)}, u32[]{:S(2)}) %copy-start.3) | copy-done | bytes 81944
  2.5 0.0 copy-done.5
  2.5 0.0 copy-start.1
  2.5 1.0 %copy-done.1 = f32[64,1,8,256]{3,2,1,0:T(8,128)S(1)} copy-done((f32[64,1,8,256]{3,2,1,0:T(8,128)S(1)}, f32[64,1,8,256]{3,2,1,0:T(8,128)}, u32[]{:S(2)}) %copy-start.1) | copy-done | bytes 524312
  3.6 0.0 copy-start.2
  3.6 1.0 %copy-done.2 = f32[64,1,8,256]{3,2,1,0:T(8,128)S(1)} copy-done((f32[64,1,8,256]{3,2,1,0:T(8,128)S(1)}, f32[64,1,8,256]{3,2,1,0:T(8,128)}, u32[]{:S(2)}) %copy-start.2) | copy-done | bytes 524312
  4.6 71.9 %shard_map.77 = (f32[8,8,8,256]{3,2,1,0:T(8,128)S(1)}, f32[8,8,8,256]{3,2,1,0:T(8,128)S(1)}) custom-call(s32[20,64]{1,0:T(8,128)S(1)} %reshape.27.part_ref, f32[20,64]{1,0:T(8,128)S(1)} %reshape.28.wt_ref, f32[64,8,256]{2,1,0:T(8,128)S(1)} %bitcast.23, f32[64,8,256]{2,1,0:T(8,128)S(1)} %bitcast.24, f32[11,8,256]{2,1,0:T(8,128)S(1)} %pad_maximum_fusion.c_ref), custom_call_target="tpu_custom_call" | custom-call | tf_op jit(solution)/shard_map/pallas_call | solution.py:250
  76.5 0.8 %copy.21 = f32[64,1,8,256]{3,2,1,0:T(8,128)} copy(f32[64,1,8,256]{3,2,1,0:T(8,128)S(1)} %bitcast.26) | data formatting | bytes 1048576
  77.3 0.8 %copy.22 = f32[64,1,8,256]{3,2,1,0:T(8,128)} copy(f32[64,1,8,256]{3,2,1,0:T(8,128)S(1)} %bitcast.25) | data formatting | bytes 1048576
  (8 shorter events, 0.1 us)
Async XLA Ops:
  0.6 0.9 %copy-start = (s32[10,256,2]{1,2,0:T(2,128)S(1)}, s32[10,256,2]{1,2,0:T(2,128)}, u32[]{:S(2)}) copy-start(s32[10,256,2]{1,2,0:T(2,128)} %param.10) | copy-start | bytes 61444
  0.6 0.7 copy-start.4
  1.6 0.9 %copy-start.3 = (f32[10,1,8,256]{3,2,1,0:T(8,128)S(1)}, f32[10,1,8,256]{3,2,1,0:T(8,128)}, u32[]{:S(2)}) copy-start(f32[10,1,8,256]{3,2,1,0:T(8,128)} %param.9) | copy-start | bytes 245764
  1.7 0.8 %copy-start.5 = (f32[1,8,256]{2,1,0:T(8,128)S(1)}, f32[1,8,256]{2,1,0:T(8,128)}, u32[]{:S(2)}) copy-start(f32[1,8,256]{2,1,0:T(8,128)} %param.8) | copy-start | bytes 24580
  2.5 1.0 %copy-start.1 = (f32[64,1,8,256]{3,2,1,0:T(8,128)S(1)}, f32[64,1,8,256]{3,2,1,0:T(8,128)}, u32[]{:S(2)}) copy-start(f32[64,1,8,256]{3,2,1,0:T(8,128)} %param.6) | copy-start | bytes 1572868
  3.6 1.0 %copy-start.2 = (f32[64,1,8,256]{3,2,1,0:T(8,128)S(1)}, f32[64,1,8,256]{3,2,1,0:T(8,128)}, u32[]{:S(2)}) copy-start(f32[64,1,8,256]{3,2,1,0:T(8,128)} %param.7) | copy-start | bytes 1572868

commit v3 on v2

--- a/solution.py
+++ b/solution.py
@@ -11,6 +11,7 @@
 MESH = pl.DeviceIdType.MESH
 VMEM = pl.BlockSpec(memory_space=pltpu.VMEM)
 SMEM = pl.BlockSpec(memory_space=pltpu.SMEM)
+HBM = pl.BlockSpec(memory_space=pltpu.HBM)
 LIMIT = 40 * 1024 * 1024
 
 
@@ -53,71 +54,122 @@
 
 
 def kernel(
-    n_gx, n_ma, chunks, pieces, part_ref, wt_ref, v_ref, src_ref, c_ref, res_ref, cor_ref,
-    all_ref, side_ref, mean_ref, f_ref, fm_ref, u_ref, qr_ref, ql_ref, from_left, from_right, trans, back,
-    s_p, r_p, s_f, r_f, s_o, r_o, s_c, r_c, s_m, r_m, s_h, r_h, s_t, r_t, s_b, r_b,
+    n_gx, n_ma, chunks, pieces, halves, part_ref, wt_ref, v_hbm, src_hbm, c0_ref, c_ref, res_ref, cor_ref,
+    all_refs, v_ref, src_ref, side_ref, mean_ref, f_ref, fm_ref, u_ref, qr_refs, ql_refs, from_left, from_right, trans, back,
+    s_p, r_p, s_f, r_f, s_o, r_o, s_c, r_c, s_m, r_m, s_h, r_h, s_t, r_t, s_b, r_b, s_in,
 ):
     gx, ma = lax.axis_index("gx"), lax.axis_index("ma")
     right, left = lax.rem(gx + 1, n_gx), lax.rem(gx + n_gx - 1, n_gx)
     modes = v_ref.shape[0]
-    fields = c_ref.shape[0]
+    fields = c_ref.shape[0] + 1
+    half = v_ref.shape[-1] // halves
     part = modes // n_gx
     sub = part // chunks
     pairs = n_ma // 2
     twin = ma + 1 - 2 * lax.rem(ma, 2)
+    inputs = [
+        pltpu.make_async_copy(v_hbm, v_ref, s_in.at[0]),
+        pltpu.make_async_copy(src_hbm, src_ref, s_in.at[1]),
+    ]
+    for copy in inputs:
+        copy.start()
     greet(gx, n_gx, ma, n_ma)
+    mine = pl.ds(ma * modes, modes)
+    lanes = [pl.ds(h * half, half) for h in range(halves)]
+    joined = lambda parts: jnp.concatenate(parts, -1) if len(parts) > 1 else parts[0]
 
     size = modes // pieces
-    far = {}
-    for p in range(pieces):
-        for d in range(1, pairs):
-            far[p, d] = remote(
-                v_ref.at[pl.ds(p * size, size)],
-                all_ref.at[pl.ds(ma * modes + p * size, size)],
-                s_p.at[p, d], r_p.at[p, d], "ma", lax.rem(ma + 2 * d, n_ma),
-            )
+    far, near = {}, {}
+    means = [
+        remote(c0_ref.at[0], mean_ref.at[gx], s_m.at[d], r_m.at[d], "gx", lax.rem(gx + d, n_gx))
+        for d in range(1, n_gx)
+    ]
     side = [
         remote(c_ref, side_ref.at[1], s_c.at[1], r_c.at[1], "gx", right),
         remote(c_ref, side_ref.at[0], s_c.at[0], r_c.at[0], "gx", left),
     ]
-    near = [remote(v_ref, all_ref.at[pl.ds(ma * modes, modes)], s_o.at[0], r_o.at[0], "ma", twin)]
-    means = [
-        remote(c_ref.at[0], mean_ref.at[gx], s_m.at[d], r_m.at[d], "gx", lax.rem(gx + d, n_gx))
-        for d in range(1, n_gx)
-    ]
-    all_ref[pl.ds(ma * modes, modes)] = v_ref[...]
-    mean_ref[gx] = c_ref[0]
-    for k in range(fields):
-        for m, face in enumerate(faces_of(c_ref[k])):
+    for h in range(halves):
+        for p in range(pieces):
+            for d in range(1, pairs):
+                far[h, p, d] = remote(
+                    v_hbm.at[pl.ds(p * size, size), :, lanes[h]],
+                    all_refs[h].at[pl.ds(ma * modes + p * size, size)],
+                    s_p.at[h, p, d], r_p.at[h, p, d], "ma", lax.rem(ma + 2 * d, n_ma),
+                )
+    for h in range(halves):
+        near[h] = [remote(v_hbm.at[:, :, lanes[h]], all_refs[h].at[mine], s_o.at[h], r_o.at[h], "ma", twin)]
+    mean_ref[gx] = c0_ref[0]
+    for k in range(1, fields):
+        for m, face in enumerate(faces_of(c_ref[k - 1])):
             f_ref[m, k] = face
-    for p in range(pieces):
-        for d in range(1, pairs):
-            far[p, d].wait()
-            rows = pl.ds(lax.rem(ma + n_ma - 2 * d, n_ma) * modes + p * size, size)
-            near.append(
-                remote(all_ref.at[rows], all_ref.at[rows], s_f.at[p, d], r_f.at[p, d], "ma", twin)
-            )
-        if p == 0:
-            for copy in side:
-                copy.wait()
-            for k in range(fields):
-                f_ref[4, k] = 0.5 * (c_ref[k] + side_ref[0, k])
-                f_ref[5, k] = 0.5 * (c_ref[k] + side_ref[1, k])
-            for copy in means:
-                copy.wait()
-            for s in range(n_gx):
-                c = mean_ref[s]
-                f = faces_of(c) + [
-                    0.5 * (c + mean_ref[(s + 1) % n_gx]),
-                    0.5 * (c + mean_ref[(s + n_gx - 1) % n_gx]),
-                ]
-                for m in range(6):
-                    fm_ref[m, s] = f[m]
-                fm_ref[6, s] = f[0] + f[1] + f[2] + f[3] + f[4] + f[5] + 1.0
-    for copy in near:
+    inputs[0].wait()
+    for h in range(halves):
+        all_refs[h][mine] = v_ref[:, :, h * half : (h + 1) * half]
+    for copy in means:
         copy.wait()
-
-    halos = []
+    for s in range(n_gx):
+        c = mean_ref[s]
+        f = faces_of(c) + [
+            0.5 * (c + mean_ref[(s + 1) % n_gx]),
+            0.5 * (c + mean_ref[(s + n_gx - 1) % n_gx]),
+        ]
+        for m in range(6):
+            fm_ref[m, s] = f[m]
+        fm_ref[6, s] = f[0] + f[1] + f[2] + f[3] + f[4] + f[5] + 1.0
+    for m in range(6):
+        f_ref[m, 0] = fm_ref[m, gx]
+    for copy in side:
+        copy.wait()
+    for k in range(1, fields):
+        f_ref[4, k] = 0.5 * (c_ref[k - 1] + side_ref[0, k - 1])
+        f_ref[5, k] = 0.5 * (c_ref[k - 1] + side_ref[1, k - 1])
+    inputs[1].wait()
+
+    halos = {}
+
+    def exchange(q, h):
+        halos[q, h] = (
+            remote(qr_refs[h].at[q], from_left[h].at[q], s_h.at[h, q, 0], r_h.at[h, q, 0], "gx", right),
+            remote(ql_refs[h].at[q], from_right[h].at[q], s_h.at[h, q, 1], r_h.at[h, q, 1], "gx", left),
+        )
+
+    for h in range(halves):
+        for p in range(pieces):
+            for d in range(1, pairs):
+                far[h, p, d].wait()
+                rows = pl.ds(lax.rem(ma + n_ma - 2 * d, n_ma) * modes + p * size, size)
+                near[h].append(
+                    remote(all_refs[h].at[rows], all_refs[h].at[rows], s_f.at[h, p, d], r_f.at[h, p, d], "ma", twin)
+                )
+        for copy in near[h]:
+            copy.wait()
+        if h + 1 == halves:
+            break
+        for q in range(chunks):
+
+            def ahead(d, carry):
+                base = d * part + q * sub
+                cut = slice(h * half, (h + 1) * half)
+                f = [f_ref[m, 0, :, cut] for m in (4, 5)]
+                sums = [[x * v_ref[base + g, :, cut] for x in f] for g in range(sub)]
+                for k in range(1, fields):
+                    row = 2 * (k - 1)
+                    f = [f_ref[m, k, :, cut] for m in (4, 5)]
+                    for g in range(sub):
+                        i = base + g
+                        value = (
+                            wt_ref[row, i] * all_refs[h][part_ref[row, i]]
+                            + wt_ref[row + 1, i] * all_refs[h][part_ref[row + 1, i]]
+                        )
+                        sums[g] = [total + x * value for total, x in zip(sums[g], f)]
+                for g in range(sub):
+                    qr_refs[h][q, d, g] = sums[g][0]
+                    ql_refs[h][q, d, g] = sums[g][1]
+                return carry
+
+            lax.fori_loop(0, n_gx, ahead, 0)
+            exchange(q, h)
+
     for q in range(chunks):
 
         def body(d, carry):
@@ -130,33 +182,34 @@
                 f = [f_ref[m, k] for m in range(6)]
                 for g in range(sub):
                     i = base + g
-                    h = wt_ref[row, i] * all_ref[part_ref[row, i]] + wt_ref[row + 1, i] * all_ref[part_ref[row + 1, i]]
+                    h = joined(
+                        [
+                            wt_ref[row, i] * ref[part_ref[row, i]] + wt_ref[row + 1, i] * ref[part_ref[row + 1, i]]
+                            for ref in all_refs
+                        ]
+                    )
                     sums[g] = [sums[g][m] + f[m] * h for m in range(6)]
             for g in range(sub):
                 t = sums[g]
                 image = values[g] + (t[0] + t[1] + t[2] + t[3] + t[4] + t[5]) - shift_faces(t)
                 u_ref[q, d, g] = src_ref[base + g] - image
-                qr_ref[q, d, g] = t[4]
-                ql_ref[q, d, g] = t[5]
+                qr_refs[-1][q, d, g] = t[4][:, (halves - 1) * half :]
+                ql_refs[-1][q, d, g] = t[5][:, (halves - 1) * half :]
             return carry
 
         lax.fori_loop(0, n_gx, body, 0)
-        halos.append(
-            (
-                remote(qr_ref.at[q], from_left.at[q], s_h.at[q, 0], r_h.at[q, 0], "gx", right),
-                remote(ql_ref.at[q], from_right.at[q], s_h.at[q, 1], r_h.at[q, 1], "gx", left),
-            )
-        )
+        exchange(q, halves - 1)
 
     moved = {}
     returned = []
 
     def settle(q):
-        for copy in halos[q]:
-            copy.wait()
+        for h in range(halves):
+            for copy in halos[q, h]:
+                copy.wait()
         cols = pl.ds(q * sub, sub)
         for d in range(n_gx):
-            res_ref[d, cols] = u_ref[q, d] + from_left[q, d] + from_right[q, d]
+            res_ref[d, cols] = u_ref[q, d] + joined([a[q, d] + b[q, d] for a, b in zip(from_left, from_right)])
         moved[q] = [
             remote(
                 res_ref.at[lax.rem(gx + d, n_gx), cols], trans.at[q, gx],
@@ -236,38 +289,44 @@
     weight = jnp.where(here != ids, strength, 0.0)
     partner = here.transpose(0, 2, 1).reshape(2 * fields, modes)
     weight = weight.transpose(0, 2, 1).reshape(2 * fields, modes)
-    stacked = jnp.concatenate([mean_conductivity, kl_fields[:, 0]], 0)
+    halves = 2 if nz % 256 == 0 else 1
     v = solution.reshape(modes, ny, nz)
     src = source.reshape(modes, ny, nz)
     part = modes // n_gx
     chunks = next(n for n in (4, 2, 1) if part % n == 0)
-    pieces = next(n for n in (4, 2, 1) if modes % n == 0)
+    pieces = next(n for n in (2, 1) if modes % n == 0)
     sub = part // chunks
     pairs = n_ma // 2
     dma = pltpu.SemaphoreType.DMA
     vmem = lambda *lead: pltpu.VMEM(lead + (ny, nz), f32)
+    split = lambda *lead: (pltpu.VMEM(lead + (ny, nz // halves), f32),) * halves
     field = jax.ShapeDtypeStruct((n_gx, part, ny, nz), f32)
     residual, correction = pl.pallas_call(
-        functools.partial(kernel, n_gx, n_ma, chunks, pieces),
+        functools.partial(kernel, n_gx, n_ma, chunks, pieces, halves),
         out_shape=(field,) * 2,
-        in_specs=[SMEM] * 2 + [VMEM] * 3,
+        in_specs=[SMEM] * 2 + [HBM] * 2 + [VMEM] * 2,
         out_specs=(VMEM,) * 2,
         scratch_shapes=[
-            vmem(n_ma * modes),
-            vmem(2, fields + 1),
+            split(n_ma * modes),
+            vmem(modes),
+            vmem(modes),
+            vmem(2, fields),
             vmem(n_gx),
             vmem(6, fields + 1),
             vmem(7, n_gx),
+            vmem(chunks, n_gx, sub),
         ]
-        + [vmem(chunks, n_gx, sub)] * 7
-        + [dma((pieces, pairs))] * 4
-        + [dma((1,))] * 2
+        + [split(chunks, n_gx, sub)] * 4
+        + [vmem(chunks, n_gx, sub)] * 2
+        + [dma((halves, pieces, pairs))] * 4
+        + [dma((halves,))] * 2
         + [dma((2,))] * 2
         + [dma((n_gx,))] * 2
-        + [dma((chunks, 2))] * 2
-        + [dma((chunks, n_gx))] * 4,
+        + [dma((halves, chunks, 2))] * 2
+        + [dma((chunks, n_gx))] * 4
+        + [dma((2,))],
         compiler_params=pltpu.CompilerParams(collective_id=0, has_side_effects=True, vmem_limit_bytes=LIMIT),
-    )(partner, weight, v, src, stacked)
+    )(partner, weight, v, src, mean_conductivity, kl_fields.reshape(fields, ny, nz))
     return residual.reshape(shape), correction.reshape(shape)
 
 

time: 78.4 us -> 74.1 us (0.945)
  Pallas kernels: 71.9 us -> 67.6 us
    pallas_call x1, Pallas kernels: 71.9 us -> 67.6 us  [shards(): pl.pallas_call(functools.partial(kernel, n_gx, n_ma, chunks, pieces, halv...]
where the time goes in v3:
time: 74.1 us; the launch traced here: 73.8 us
  Pallas kernels  67.6 us (91%)
  local copies, waits for them, and re-layouts  5.29 us (7%)
    pallas_call x1, Pallas kernels, shards(): pl.pallas_call(functools.partial(kernel, n_gx, n_ma, chunks, pieces, halv...  67.6 us
    unnamed x15, local copies, waits for them, and re-layouts  5.17 us

profile of v3, /device:TPU:0, one launch (start us, length us, event | category | flops | bytes accessed | tf_op | source)
XLA Modules:
  0.0 73.8 jit_solution(15357049255402265748)
XLA Ops:
  0.6 0.0 copy-start
  0.6 0.0 copy-start.5
  0.7 0.7 copy-done.5
  1.4 0.1 convert_bitcast_fusion
  1.4 0.1 fusion.2
  1.5 0.0 copy-done
  1.5 0.1 constant_dynamic-slice_fusion
  1.6 0.0 copy-start.3
  1.7 0.0 copy-start.4
  1.7 0.8 %copy-done.3 = f32[10,1,8,256]{3,2,1,0:T(8,128)S(1)} copy-done((f32[10,1,8,256]{3,2,1,0:T(8,128)S(1)}, f32[10,1,8,256]{3,2,1,0:T(8,128)}, u32[]{:S(2)}) %copy-start.3) | copy-done | bytes 81944
  2.5 0.0 copy-done.4
  2.5 0.0 copy-start.1
  2.5 1.0 %copy-done.1 = f32[64,1,8,256]{3,2,1,0:T(8,128)S(1)} copy-done((f32[64,1,8,256]{3,2,1,0:T(8,128)S(1)}, f32[64,1,8,256]{3,2,1,0:T(8,128)}, u32[]{:S(2)}) %copy-start.1) | copy-done | bytes 524312
  3.5 0.0 copy-start.2
  3.5 1.0 %copy-done.2 = f32[64,1,8,256]{3,2,1,0:T(8,128)S(1)} copy-done((f32[64,1,8,256]{3,2,1,0:T(8,128)S(1)}, f32[64,1,8,256]{3,2,1,0:T(8,128)}, u32[]{:S(2)}) %copy-start.2) | copy-done | bytes 524312
  4.6 67.6 %shard_map.77 = (f32[8,8,8,256]{3,2,1,0:T(8,128)S(1)}, f32[8,8,8,256]{3,2,1,0:T(8,128)S(1)}) custom-call(s32[20,64]{1,0:T(8,128)S(1)} %reshape.30.part_ref, f32[20,64]{1,0:T(8,128)S(1)} %reshape.31.wt_ref, f32[64,8,256]{2,1,0:T(8,128)S(1)} %bitcast.23, f32[64,8,256]{2,1,0:T(8,128)S(1)} %bitcast.24, f32[1,8,256]{2,1,0:T(8,128)S(1)} %copy-done.4, ...), custom_call_target="tpu_custom_call" | custom-call | tf_op jit(solution)/shard_map/pallas_call | solution.py:304
  72.2 0.8 %copy.21 = f32[64,1,8,256]{3,2,1,0:T(8,128)} copy(f32[64,1,8,256]{3,2,1,0:T(8,128)S(1)} %bitcast.26) | data formatting | bytes 1048576
  73.0 0.8 %copy.22 = f32[64,1,8,256]{3,2,1,0:T(8,128)} copy(f32[64,1,8,256]{3,2,1,0:T(8,128)S(1)} %bitcast.25) | data formatting | bytes 1048576
  (7 shorter events, 0.1 us)
Async XLA Ops:
  0.6 0.9 %copy-start = (s32[10,256,2]{1,2,0:T(2,128)S(1)}, s32[10,256,2]{1,2,0:T(2,128)}, u32[]{:S(2)}) copy-start(s32[10,256,2]{1,2,0:T(2,128)} %param.10) | copy-start | bytes 61444
  0.6 0.7 copy-start.5
  1.6 0.9 %copy-start.3 = (f32[10,1,8,256]{3,2,1,0:T(8,128)S(1)}, f32[10,1,8,256]{3,2,1,0:T(8,128)}, u32[]{:S(2)}) copy-start(f32[10,1,8,256]{3,2,1,0:T(8,128)} %param.9) | copy-start | bytes 245764
  1.7 0.8 %copy-start.4 = (f32[1,8,256]{2,1,0:T(8,128)S(1)}, f32[1,8,256]{2,1,0:T(8,128)}, u32[]{:S(2)}) copy-start(f32[1,8,256]{2,1,0:T(8,128)} %c0_ref.1) | copy-start | bytes 24580
  2.5 1.0 %copy-start.1 = (f32[64,1,8,256]{3,2,1,0:T(8,128)S(1)}, f32[64,1,8,256]{3,2,1,0:T(8,128)}, u32[]{:S(2)}) copy-start(f32[64,1,8,256]{3,2,1,0:T(8,128)} %param.6) | copy-start | bytes 1572868
  3.5 1.0 %copy-start.2 = (f32[64,1,8,256]{3,2,1,0:T(8,128)S(1)}, f32[64,1,8,256]{3,2,1,0:T(8,128)}, u32[]{:S(2)}) copy-start(f32[64,1,8,256]{3,2,1,0:T(8,128)} %param.7) | copy-start | bytes 1572868

commit v4 on v3

--- a/solution.py
+++ b/solution.py
@@ -266,10 +266,9 @@
             )
         cor_ref[gx, cols] = back[q, gx]
 
-    settle(0)
     for q in range(chunks):
-        if q + 1 < chunks:
-            settle(q + 1)
+        settle(q)
+    for q in range(chunks):
         polish(q)
     for copy in returned:
         copy.wait()

time: 74.1 us -> 69.7 us (0.941)
  Pallas kernels: 67.6 us -> 63.2 us
    pallas_call x1, Pallas kernels: 67.6 us -> 63.2 us  [shards(): pl.pallas_call(functools.partial(kernel, n_gx, n_ma, chunks, pieces, halv...]
where the time goes in v4:
time: 69.7 us; the launch traced here: 69.4 us
  Pallas kernels  63.2 us (91%)
  local copies, waits for them, and re-layouts  5.29 us (8%)
  between operations  0.72 us (1%)
    pallas_call x1, Pallas kernels, shards(): pl.pallas_call(functools.partial(kernel, n_gx, n_ma, chunks, pieces, halv...  63.2 us
    unnamed x15, local copies, waits for them, and re-layouts  5.17 us

profile of v4, /device:TPU:0, one launch (start us, length us, event | category | flops | bytes accessed | tf_op | source)
XLA Modules:
  0.0 69.4 jit_solution(6626960441594753375)
XLA Ops:
  0.6 0.0 copy-start
  0.6 0.0 copy-start.5
  0.7 0.7 %copy-done.5 = s32[256,10]{0,1:T(8,128)S(1)} copy-done((s32[256,10]{0,1:T(8,128)S(1)}, s32[256,10]{0,1:T(8,128)}, u32[]{:S(2)}) %copy-start.5) | copy-done | bytes 10264
  1.4 0.1 convert_bitcast_fusion
  1.4 0.1 fusion.2
  1.5 0.0 copy-done
  1.5 0.1 constant_dynamic-slice_fusion
  1.6 0.0 copy-start.3
  1.7 0.0 copy-start.4
  1.7 0.8 %copy-done.3 = f32[10,1,8,256]{3,2,1,0:T(8,128)S(1)} copy-done((f32[10,1,8,256]{3,2,1,0:T(8,128)S(1)}, f32[10,1,8,256]{3,2,1,0:T(8,128)}, u32[]{:S(2)}) %copy-start.3) | copy-done | bytes 81944
  2.5 0.0 copy-done.4
  2.5 0.0 copy-start.1
  2.5 1.0 %copy-done.1 = f32[64,1,8,256]{3,2,1,0:T(8,128)S(1)} copy-done((f32[64,1,8,256]{3,2,1,0:T(8,128)S(1)}, f32[64,1,8,256]{3,2,1,0:T(8,128)}, u32[]{:S(2)}) %copy-start.1) | copy-done | bytes 524312
  3.5 0.0 copy-start.2
  3.5 1.0 %copy-done.2 = f32[64,1,8,256]{3,2,1,0:T(8,128)S(1)} copy-done((f32[64,1,8,256]{3,2,1,0:T(8,128)S(1)}, f32[64,1,8,256]{3,2,1,0:T(8,128)}, u32[]{:S(2)}) %copy-start.2) | copy-done | bytes 524312
  4.6 63.2 %shard_map.77 = (f32[8,8,8,256]{3,2,1,0:T(8,128)S(1)}, f32[8,8,8,256]{3,2,1,0:T(8,128)S(1)}) custom-call(s32[20,64]{1,0:T(8,128)S(1)} %reshape.30.part_ref, f32[20,64]{1,0:T(8,128)S(1)} %reshape.31.wt_ref, f32[64,8,256]{2,1,0:T(8,128)S(1)} %bitcast.23, f32[64,8,256]{2,1,0:T(8,128)S(1)} %bitcast.24, f32[1,8,256]{2,1,0:T(8,128)S(1)} %copy-done.4, ...), custom_call_target="tpu_custom_call" | custom-call | tf_op jit(solution)/shard_map/pallas_call | solution.py:303
  67.8 0.8 %copy.21 = f32[64,1,8,256]{3,2,1,0:T(8,128)} copy(f32[64,1,8,256]{3,2,1,0:T(8,128)S(1)} %bitcast.26) | data formatting | bytes 1048576
  68.6 0.8 %copy.22 = f32[64,1,8,256]{3,2,1,0:T(8,128)} copy(f32[64,1,8,256]{3,2,1,0:T(8,128)S(1)} %bitcast.25) | data formatting | bytes 1048576
  (7 shorter events, 0.1 us)
Async XLA Ops:
  0.6 0.9 %copy-start = (s32[10,256,2]{1,2,0:T(2,128)S(1)}, s32[10,256,2]{1,2,0:T(2,128)}, u32[]{:S(2)}) copy-start(s32[10,256,2]{1,2,0:T(2,128)} %param.10) | copy-start | bytes 61444
  0.6 0.7 %copy-start.5 = (s32[256,10]{0,1:T(8,128)S(1)}, s32[256,10]{0,1:T(8,128)}, u32[]{:S(2)}) copy-start(s32[256,10]{0,1:T(8,128)} %param.11) | copy-start | bytes 30724
  1.6 0.9 %copy-start.3 = (f32[10,1,8,256]{3,2,1,0:T(8,128)S(1)}, f32[10,1,8,256]{3,2,1,0:T(8,128)}, u32[]{:S(2)}) copy-start(f32[10,1,8,256]{3,2,1,0:T(8,128)} %param.9) | copy-start | bytes 245764
  1.7 0.8 %copy-start.4 = (f32[1,8,256]{2,1,0:T(8,128)S(1)}, f32[1,8,256]{2,1,0:T(8,128)}, u32[]{:S(2)}) copy-start(f32[1,8,256]{2,1,0:T(8,128)} %c0_ref.1) | copy-start | bytes 24580
  2.5 1.0 %copy-start.1 = (f32[64,1,8,256]{3,2,1,0:T(8,128)S(1)}, f32[64,1,8,256]{3,2,1,0:T(8,128)}, u32[]{:S(2)}) copy-start(f32[64,1,8,256]{3,2,1,0:T(8,128)} %param.6) | copy-start | bytes 1572868
  3.5 1.0 %copy-start.2 = (f32[64,1,8,256]{3,2,1,0:T(8,128)S(1)}, f32[64,1,8,256]{3,2,1,0:T(8,128)}, u32[]{:S(2)}) copy-start(f32[64,1,8,256]{3,2,1,0:T(8,128)} %param.7) | copy-start | bytes 1572868

commit v5 on v4

--- a/solution.py
+++ b/solution.py
@@ -88,7 +88,7 @@
         remote(c_ref, side_ref.at[1], s_c.at[1], r_c.at[1], "gx", right),
         remote(c_ref, side_ref.at[0], s_c.at[0], r_c.at[0], "gx", left),
     ]
-    for h in range(halves):
+    def send(h):
         for p in range(pieces):
             for d in range(1, pairs):
                 far[h, p, d] = remote(
@@ -96,8 +96,9 @@
                     all_refs[h].at[pl.ds(ma * modes + p * size, size)],
                     s_p.at[h, p, d], r_p.at[h, p, d], "ma", lax.rem(ma + 2 * d, n_ma),
                 )
-    for h in range(halves):
         near[h] = [remote(v_hbm.at[:, :, lanes[h]], all_refs[h].at[mine], s_o.at[h], r_o.at[h], "ma", twin)]
+
+    send(0)
     mean_ref[gx] = c0_ref[0]
     for k in range(1, fields):
         for m, face in enumerate(faces_of(c_ref[k - 1])):
@@ -141,6 +142,8 @@
                 near[h].append(
                     remote(all_refs[h].at[rows], all_refs[h].at[rows], s_f.at[h, p, d], r_f.at[h, p, d], "ma", twin)
                 )
+        if h + 1 < halves:
+            send(h + 1)
         for copy in near[h]:
             copy.wait()
         if h + 1 == halves:

time: 69.7 us -> 68.5 us (0.983)
  Pallas kernels: 63.2 us -> 62 us
    pallas_call x1, Pallas kernels: 63.2 us -> 62 us  [shards(): pl.pallas_call(functools.partial(kernel, n_gx, n_ma, chunks, pieces, halv...]
where the time goes in v5:
time: 68.5 us; the launch traced here: 68.2 us
  Pallas kernels  62 us (91%)
  local copies, waits for them, and re-layouts  5.29 us (8%)
  between operations  0.72 us (1%)
    pallas_call x1, Pallas kernels, shards(): pl.pallas_call(functools.partial(kernel, n_gx, n_ma, chunks, pieces, halv...  62 us
    unnamed x15, local copies, waits for them, and re-layouts  5.17 us

profile of v5, /device:TPU:0, one launch (start us, length us, event | category | flops | bytes accessed | tf_op | source)
XLA Modules:
  0.0 68.2 jit_solution(9772733042823218395)
XLA Ops:
  0.6 0.0 copy-start
  0.6 0.0 copy-start.5
  0.7 0.7 %copy-done.5 = s32[256,10]{0,1:T(8,128)S(1)} copy-done((s32[256,10]{0,1:T(8,128)S(1)}, s32[256,10]{0,1:T(8,128)}, u32[]{:S(2)}) %copy-start.5) | copy-done | bytes 10264
  1.4 0.1 convert_bitcast_fusion
  1.4 0.1 fusion.2
  1.5 0.0 copy-done
  1.5 0.1 constant_dynamic-slice_fusion
  1.6 0.0 copy-start.3
  1.7 0.0 copy-start.4
  1.7 0.8 %copy-done.3 = f32[10,1,8,256]{3,2,1,0:T(8,128)S(1)} copy-done((f32[10,1,8,256]{3,2,1,0:T(8,128)S(1)}, f32[10,1,8,256]{3,2,1,0:T(8,128)}, u32[]{:S(2)}) %copy-start.3) | copy-done | bytes 81944
  2.5 0.0 copy-done.4
  2.5 0.0 copy-start.1
  2.5 1.0 %copy-done.1 = f32[64,1,8,256]{3,2,1,0:T(8,128)S(1)} copy-done((f32[64,1,8,256]{3,2,1,0:T(8,128)S(1)}, f32[64,1,8,256]{3,2,1,0:T(8,128)}, u32[]{:S(2)}) %copy-start.1) | copy-done | bytes 524312
  3.5 0.0 copy-start.2
  3.5 1.0 %copy-done.2 = f32[64,1,8,256]{3,2,1,0:T(8,128)S(1)} copy-done((f32[64,1,8,256]{3,2,1,0:T(8,128)S(1)}, f32[64,1,8,256]{3,2,1,0:T(8,128)}, u32[]{:S(2)}) %copy-start.2) | copy-done | bytes 524312
  4.6 62.0 %shard_map.77 = (f32[8,8,8,256]{3,2,1,0:T(8,128)S(1)}, f32[8,8,8,256]{3,2,1,0:T(8,128)S(1)}) custom-call(s32[20,64]{1,0:T(8,128)S(1)} %reshape.30.part_ref, f32[20,64]{1,0:T(8,128)S(1)} %reshape.31.wt_ref, f32[64,8,256]{2,1,0:T(8,128)S(1)} %bitcast.23, f32[64,8,256]{2,1,0:T(8,128)S(1)} %bitcast.24, f32[1,8,256]{2,1,0:T(8,128)S(1)} %copy-done.4, ...), custom_call_target="tpu_custom_call" | custom-call | tf_op jit(solution)/shard_map/pallas_call | solution.py:306
  66.6 0.8 %copy.21 = f32[64,1,8,256]{3,2,1,0:T(8,128)} copy(f32[64,1,8,256]{3,2,1,0:T(8,128)S(1)} %bitcast.26) | data formatting | bytes 1048576
  67.4 0.8 %copy.22 = f32[64,1,8,256]{3,2,1,0:T(8,128)} copy(f32[64,1,8,256]{3,2,1,0:T(8,128)S(1)} %bitcast.25) | data formatting | bytes 1048576
  (7 shorter events, 0.1 us)
Async XLA Ops:
  0.6 0.9 %copy-start = (s32[10,256,2]{1,2,0:T(2,128)S(1)}, s32[10,256,2]{1,2,0:T(2,128)}, u32[]{:S(2)}) copy-start(s32[10,256,2]{1,2,0:T(2,128)} %param.10) | copy-start | bytes 61444
  0.6 0.7 %copy-start.5 = (s32[256,10]{0,1:T(8,128)S(1)}, s32[256,10]{0,1:T(8,128)}, u32[]{:S(2)}) copy-start(s32[256,10]{0,1:T(8,128)} %param.11) | copy-start | bytes 30724
  1.6 0.9 %copy-start.3 = (f32[10,1,8,256]{3,2,1,0:T(8,128)S(1)}, f32[10,1,8,256]{3,2,1,0:T(8,128)}, u32[]{:S(2)}) copy-start(f32[10,1,8,256]{3,2,1,0:T(8,128)} %param.9) | copy-start | bytes 245764
  1.7 0.8 %copy-start.4 = (f32[1,8,256]{2,1,0:T(8,128)S(1)}, f32[1,8,256]{2,1,0:T(8,128)}, u32[]{:S(2)}) copy-start(f32[1,8,256]{2,1,0:T(8,128)} %c0_ref.1) | copy-start | bytes 24580
  2.5 1.0 %copy-start.1 = (f32[64,1,8,256]{3,2,1,0:T(8,128)S(1)}, f32[64,1,8,256]{3,2,1,0:T(8,128)}, u32[]{:S(2)}) copy-start(f32[64,1,8,256]{3,2,1,0:T(8,128)} %param.6) | copy-start | bytes 1572868
  3.5 1.0 %copy-start.2 = (f32[64,1,8,256]{3,2,1,0:T(8,128)S(1)}, f32[64,1,8,256]{3,2,1,0:T(8,128)}, u32[]{:S(2)}) copy-start(f32[64,1,8,256]{3,2,1,0:T(8,128)} %param.7) | copy-start | bytes 1572868
